TPU v7x, 32 devices: a whole 2x2x4 slice. The times are simulated.
32 devices in a mesh: dp: 2 (over core), ctx: 8 (over z, x), head: 2 (over y).
Axes of the slice: x: 2, y: 2, z: 4, core: 2. Of those that a mesh axis runs over, the one named last changes fastest.
Arguments:
- query: bfloat16 [2, 8, 2, 512, 512], P('dp', 'ctx', 'head'), may hold values from -120 to 120
- key: bfloat16 [2, 1024, 4096], P('dp', 'ctx', 'head'), may hold values from -8 to 8
- value: bfloat16 [2, 1024, 4096], P('dp', 'ctx', 'head'), may hold values from -6 to 6
- grad_out: bfloat16 [2, 8, 2, 512, 512], P('dp', 'ctx', 'head'), may hold values from -6 to 6
- chosen: int32 [2, 2, 32, 3], P('dp', None, 'head'), may hold values from 0 to 1, as said below
- placed: int32 [2], replicated, may hold values from 0 to 1, each once
- sink: float32 [32], P('head'), may hold values from -2 to 6
Outputs:
- attended: bfloat16 [2, 8, 2, 512, 512], P('dp', 'ctx', 'head')
- grad_query: bfloat16 [2, 8, 2, 512, 512], P('dp', 'ctx', 'head')
- grad_key: bfloat16 [2, 1024, 4096], P('dp', 'ctx', 'head')
- grad_value: bfloat16 [2, 1024, 4096], P('dp', 'ctx', 'head')
- grad_sink: float32 [32], replicated
Inputs may be any that keep to these rules, and one draw needn't show every extreme that they name: `chosen`: for each sequence, block b and head, the first min(b, 3) entries are distinct blocks before b; the remaining entries are blocks from b to 1. `placed`: every block is held by exactly one slot.
All inputs are finite; a program needn't handle non-finite values.
Results may differ from a plain program's by a relative error of at most 0.025.
Values may be sent and summed in bfloat16 or wider, within the bound.
A program may use at most 64 MiB of HBM per device.

v0:
```python
import functools
import math

import jax
import jax.numpy as jnp
from jax import lax
from jax.experimental import pallas as pl
from jax.experimental.pallas import tpu as pltpu
from jax.sharding import PartitionSpec as P

HEADS = 32
DH = 128


def inner_rows(left, right):
    return lax.dot_general(
        left, right, (((1,), (1,)), ((), ())), preferred_element_type=jnp.float32
    )


def outer_rows(left, right):
    return lax.dot_general(
        left, right, (((0,), (0,)), ((), ())), preferred_element_type=jnp.float32
    )


def attend_block(query_rows, grad_rows, tiles, usable, sink_logit):
    rows, width = query_rows.shape
    scale = 1.0 / math.sqrt(width)
    keys = tiles[:, :, :width].reshape(-1, width)
    vals = tiles[:, :, width:].reshape(-1, width)
    scores = inner_rows(query_rows, keys) * scale
    cols = tiles.shape[0] * rows
    tile_of = jnp.arange(cols) // rows
    offset = jnp.arange(cols) % rows
    own_ok = offset[None, :] <= jnp.arange(rows)[:, None]
    allowed = jnp.where(tile_of[None, :] == 0, own_ok, usable[tile_of][None, :])
    masked = jnp.where(allowed, scores, -jnp.inf)
    top = jnp.maximum(jnp.max(masked, axis=1), sink_logit)
    expo = jnp.exp(masked - top[:, None])
    sink_part = jnp.exp(sink_logit - top)
    total = sink_part + jnp.sum(expo, axis=1)
    prob = expo / total[:, None]
    weights = prob.astype(jnp.bfloat16)
    attended = jnp.dot(weights, vals, preferred_element_type=jnp.float32).astype(jnp.bfloat16)
    stored = lax.optimization_barrier(attended)
    delta = jnp.sum(grad_rows.astype(jnp.float32) * stored.astype(jnp.float32), axis=1)
    dprob = inner_rows(grad_rows, vals)
    dscore = (prob * (dprob - delta[:, None]) * scale).astype(jnp.bfloat16)
    grad_query = jnp.dot(dscore, keys, preferred_element_type=jnp.float32).astype(jnp.bfloat16)
    grad_keys = outer_rows(dscore, query_rows).astype(jnp.bfloat16)
    grad_vals = outer_rows(weights, grad_rows).astype(jnp.bfloat16)
    tiles_grad = jnp.concatenate([grad_keys, grad_vals], axis=1).reshape(tiles.shape)
    sink_grad = -jnp.sum(sink_part / total * delta)
    return (attended, grad_query, tiles_grad, sink_grad)


def general_body(query, key, value, grad_out, chosen, placed, sink):
    seqs = query.shape[0]
    block = query.shape[3]
    width = DH
    hpd = query.shape[4] // width
    unit = key.shape[1]
    parts_per = block // unit
    n_ctx = lax.axis_size("ctx")
    nblk = n_ctx // parts_per
    place = lax.axis_index("ctx")
    slot = place // parts_per
    position = place % parts_per
    slots = jnp.arange(nblk, dtype=jnp.int32)
    seq_block = jnp.sum(jnp.where(slots == slot, placed, 0))
    slot_of = jnp.sum(jnp.where(placed[None, :] == slots[:, None], slots[None, :], 0), axis=1)
    mine = lax.dynamic_slice_in_dim(chosen, seq_block, 1, 1)[:, 0]
    mine = lax.dynamic_slice_in_dim(mine, position * hpd, hpd, 1)
    usable_pick = mine < seq_block
    mapped = jnp.sum(jnp.where(mine[..., None] == slots, slot_of, 0), axis=-1)
    mapped = jnp.where(usable_pick, mapped, slot)
    lead = jnp.broadcast_to(slot, mine.shape[:2] + (1,))
    picks = jnp.concatenate([lead, mapped], axis=-1)
    kinds = picks.shape[-1]
    usable = jnp.concatenate([jnp.ones(mine.shape[:2] + (1,), bool), usable_pick], axis=-1)
    sink_mine = lax.dynamic_slice_in_dim(sink, position * hpd, hpd)
    paired = jnp.concatenate(
        [
            key.reshape(seqs, unit, parts_per, hpd, width),
            value.reshape(seqs, unit, parts_per, hpd, width),
        ],
        axis=-1,
    )
    paired = jnp.transpose(paired, (2, 0, 3, 1, 4))
    items = seqs * hpd
    frag = unit * 2 * width // n_ctx
    seq_ix = jnp.arange(seqs, dtype=jnp.int32)[None, :, None, None, None]
    head_ix = jnp.arange(hpd, dtype=jnp.int32)[None, None, :, None, None]
    spread = jnp.transpose(paired.reshape(parts_per, seqs, hpd, n_ctx, frag), (3, 0, 1, 2, 4))
    held = lax.all_to_all(spread, "ctx", split_axis=0, concat_axis=0, tiled=True)
    held = jnp.transpose(held, (2, 3, 0, 1, 4)).reshape(seqs, hpd, n_ctx * parts_per, frag)
    match_block = placed[:, None] == slots[None, :]
    chosen_all = jnp.sum(jnp.where(match_block[None, :, :, None, None], chosen[:, None], 0), axis=2)
    before = chosen_all < placed[None, :, None, None]
    mapped_all = jnp.sum(jnp.where(chosen_all[..., None] == slots, slot_of, 0), axis=-1)
    own_slot = slots[None, :, None, None]
    mapped_all = jnp.where(before, mapped_all, own_slot)
    lead_all = jnp.broadcast_to(own_slot, mapped_all.shape[:3] + (1,))
    picks_all = jnp.concatenate([lead_all, mapped_all], axis=-1)
    picks_all = jnp.transpose(
        picks_all.reshape(seqs, nblk, parts_per, hpd, kinds), (1, 2, 0, 3, 4)
    ).reshape(n_ctx, seqs, hpd, kinds)
    dest_group = (jnp.arange(n_ctx, dtype=jnp.int32) % parts_per)[:, None, None, None, None]
    part_ids = jnp.arange(parts_per, dtype=jnp.int32)[None, None, None, None, :]
    route = (picks_all[..., None] * parts_per + part_ids) * parts_per + dest_group
    outgoing = held[seq_ix, head_ix, route]
    fetched = lax.all_to_all(outgoing, "ctx", split_axis=0, concat_axis=0, tiled=True)
    tiles_items = jnp.transpose(fetched, (1, 2, 3, 4, 0, 5)).reshape(
        items, kinds, parts_per * unit, 2 * width
    )
    query_heads = jnp.transpose(query.reshape(seqs, block, hpd, width), (0, 2, 1, 3)).reshape(
        items, block, width
    )
    grad_heads = jnp.transpose(grad_out.reshape(seqs, block, hpd, width), (0, 2, 1, 3)).reshape(
        items, block, width
    )
    sink_items = jnp.tile(sink_mine, seqs)

    def per_head(item):
        q_rows, g_rows, tiles, use_row, sink_logit = item
        return attend_block(q_rows, g_rows, tiles, use_row, sink_logit)

    atts, grads_q, tiles_grad, sink_grads = lax.map(
        per_head, (query_heads, grad_heads, tiles_items, usable.reshape(items, -1), sink_items)
    )
    attended = jnp.transpose(atts.reshape(seqs, hpd, block, width), (0, 2, 1, 3)).reshape(
        seqs, 1, 1, block, hpd * width
    )
    grad_query = jnp.transpose(grads_q.reshape(seqs, hpd, block, width), (0, 2, 1, 3)).reshape(
        seqs, 1, 1, block, hpd * width
    )
    shards = tiles_grad.reshape(seqs, hpd, kinds, parts_per, n_ctx, frag)
    sendback = jnp.transpose(shards, (4, 0, 1, 2, 3, 5))
    landed = lax.all_to_all(sendback, "ctx", split_axis=0, concat_axis=0, tiled=True)
    pooled = (
        jnp.zeros((seqs, hpd, n_ctx * parts_per, frag), jnp.float32)
        .at[seq_ix, head_ix, route]
        .add(landed.astype(jnp.float32))
    )
    pooled = jnp.transpose(pooled.reshape(seqs, hpd, n_ctx, parts_per, frag), (2, 3, 0, 1, 4))
    homed = lax.all_to_all(
        pooled.astype(jnp.bfloat16), "ctx", split_axis=0, concat_axis=0, tiled=True
    ).astype(pooled.dtype)
    totals = jnp.transpose(homed, (1, 2, 3, 0, 4)).reshape(parts_per, seqs, hpd, unit, 2 * width)
    totals = jnp.transpose(totals, (1, 3, 0, 2, 4))
    grad_key = totals[..., :width].reshape(seqs, unit, parts_per * hpd * width).astype(jnp.bfloat16)
    grad_value = (
        totals[..., width:].reshape(seqs, unit, parts_per * hpd * width).astype(jnp.bfloat16)
    )
    sink_local = jnp.sum(sink_grads.reshape(seqs, hpd), axis=0)
    start = lax.axis_index("head") * (parts_per * hpd) + position * hpd
    spread_sink = lax.dynamic_update_slice(jnp.zeros((HEADS,), jnp.float32), sink_local, (start,))
    grad_sink = lax.psum(spread_sink, ("dp", "ctx", "head"))
    return (attended, grad_query, grad_key, grad_value, grad_sink)


MESH = pl.DeviceIdType.MESH
ROWS = 256


def two_block_kernel(
    first, parts, hpd, unit,
    q_ref, g_ref, k_ref, v_ref, chosen_ref, sink_ref,
    att_ref, gq_ref, gk_ref, gv_ref, gs_ref,
    keys, vals, key_part, val_part, key_home, val_home, key_sum, val_sum,
    sink_part, sink_ctx, sink_peer,
    in_send, in_recv, out_send, out_recv, sink_send, sink_recv, peer_send, peer_recv,
):
    width = DH
    block = parts * unit
    scale = 1.0 / math.sqrt(width)
    me = lax.axis_index("ctx")
    slot = me // parts
    pos = me % parts
    other = 1 - slot
    is_first = slot == first
    n_ctx = 2 * parts
    mates = [slot * parts + (pos + d) % parts for d in range(1, parts)]
    across = [other * parts + (pos + d) % parts for d in range(parts)]
    peers = [ax for ax in ("head", "dp") if lax.axis_size(ax) > 1]

    barrier = pltpu.get_barrier_semaphore()
    for target in mates + across:
        pl.semaphore_signal(barrier, inc=1, device_id={"ctx": target}, device_id_type=MESH)
    for ax in peers:
        pl.semaphore_signal(barrier, inc=1, device_id={ax: 1 - lax.axis_index(ax)}, device_id_type=MESH)
    pl.semaphore_wait(barrier, n_ctx - 1 + len(peers))

    def cols(at):
        return pl.ds(pl.multiple_of(at * width, width), width)

    def fetch(h, target, source, which):
        src = (k_ref, v_ref)[which]
        dst = (keys, vals)[which]
        return pltpu.make_async_remote_copy(
            src_ref=src.at[:, cols((target % parts) * hpd + h)],
            dst_ref=dst.at[h, source],
            send_sem=in_send.at[which, h, target],
            recv_sem=in_recv.at[which, h, source],
            device_id={"ctx": target},
            device_id_type=MESH,
        )

    def give(h, target, source, which):
        src = (key_part, val_part)[which]
        dst = (key_home, val_home)[which]
        return pltpu.make_async_remote_copy(
            src_ref=src.at[h, target],
            dst_ref=dst.at[h, source],
            send_sem=out_send.at[which, h, target],
            recv_sem=out_recv.at[which, h, source],
            device_id={"ctx": target},
            device_id_type=MESH,
        )

    def each(h, targets, make, act):
        for target in targets:
            for which in range(2):
                if act == "start":
                    make(h, target, me, which).start()
                elif act == "sent":
                    make(h, target, me, which).wait_send()
                else:
                    make(h, me, target, which).wait_recv()

    @pl.when(is_first)
    def _():
        each(0, across, fetch, "start")

    def send_head(h, carry):
        each(h, mates, fetch, "start")
        keys[h, me] = k_ref[:, cols(pos * hpd + h)]
        vals[h, me] = v_ref[:, cols(pos * hpd + h)]
        return carry

    lax.fori_loop(0, hpd, send_head, 0)

    lane = lax.broadcasted_iota(jnp.int32, (8, width), 1)
    top_row = lax.broadcasted_iota(jnp.int32, (8, width), 0) == 0
    sink_part[...] = jnp.zeros((8, width), jnp.float32)

    def attend(h, with_other):
        local_head = pos * hpd + h
        k_own = keys[h, pl.ds(slot * parts, parts)].reshape(block, width)
        v_own = vals[h, pl.ds(slot * parts, parts)].reshape(block, width)
        sink_logit = sink_ref[local_head]
        segs = [(k_own, v_own, 0)]
        if with_other:
            k_oth = keys[h, pl.ds(other * parts, parts)].reshape(block, width)
            v_oth = vals[h, pl.ds(other * parts, parts)].reshape(block, width)
            segs.append((k_oth, v_oth, 1))
            sees = chosen_ref[0, 1, local_head, 0] < 1
            for entry in range(1, chosen_ref.shape[3]):
                sees = jnp.logical_or(sees, chosen_ref[0, 1, local_head, entry] < 1)
            hide = jnp.where(sees, 0.0, -jnp.inf).astype(jnp.float32)
        sink_total = jnp.zeros((1, 1), jnp.float32)
        for r in range(block // ROWS):
            rows = pl.ds(r * ROWS, ROWS)
            q = q_ref[rows, cols(h)]
            g = g_ref[rows, cols(h)]
            used = []
            top = jnp.full((ROWS, 1), sink_logit, jnp.float32)
            for k_all, v_all, kind in segs:
                n = (r + 1) * ROWS if kind == 0 else block
                k, v = k_all[:n], v_all[:n]
                s = inner_rows(q, k) * scale
                if kind == 0:
                    at_row = lax.broadcasted_iota(jnp.int32, (ROWS, n), 0) + r * ROWS
                    at_col = lax.broadcasted_iota(jnp.int32, (ROWS, n), 1)
                    s = jnp.where(at_col <= at_row, s, -jnp.inf)
                else:
                    s = s + hide
                top = jnp.maximum(top, jnp.max(s, axis=1, keepdims=True))
                used.append((k, v, s, kind, n))
            sink_exp = jnp.exp(sink_logit - top)
            total = sink_exp
            expos = []
            for k, v, s, kind, n in used:
                e = jnp.exp(s - top)
                total = total + jnp.sum(e, axis=1, keepdims=True)
                expos.append(e)
            inv = 1.0 / total
            out = jnp.zeros((ROWS, width), jnp.float32)
            probs, weights = [], []
            for (k, v, s, kind, n), e in zip(used, expos):
                p = e * inv
                w = p.astype(jnp.bfloat16)
                out = out + jnp.dot(w, v, preferred_element_type=jnp.float32)
                probs.append(p)
                weights.append(w)
            out = out.astype(jnp.bfloat16)
            att_ref[rows, cols(h)] = out
            delta = jnp.sum(g.astype(jnp.float32) * out.astype(jnp.float32), axis=1, keepdims=True)
            sink_total = sink_total - jnp.sum(sink_exp * inv * delta, axis=0, keepdims=True)
            gq = jnp.zeros((ROWS, width), jnp.float32)
            for (k, v, s, kind, n), p, w in zip(used, probs, weights):
                dprob = inner_rows(g, v)
                ds = (p * (dprob - delta) * scale).astype(jnp.bfloat16)
                gq = gq + jnp.dot(ds, k, preferred_element_type=jnp.float32)
                dk = outer_rows(ds, q)
                dv = outer_rows(w, g)
                if r == 0:
                    key_sum[kind, :n] = dk
                    val_sum[kind, :n] = dv
                    if n < block:
                        key_sum[kind, n:] = jnp.zeros((block - n, width), jnp.float32)
                        val_sum[kind, n:] = jnp.zeros((block - n, width), jnp.float32)
                else:
                    key_sum[kind, :n] += dk
                    val_sum[kind, :n] += dv
            gq_ref[rows, cols(h)] = gq.astype(jnp.bfloat16)
        mine = jnp.logical_and(lane == lax.axis_index("head") * (parts * hpd) + local_head, top_row)
        sink_part[...] += jnp.where(mine, sink_total, 0.0)
        for kind, place in ((0, slot), (1, other))[: 2 if with_other else 1]:
            at = pl.ds(place * parts, parts)
            key_part[h, at] = key_sum[kind].astype(jnp.bfloat16).reshape(parts, unit, width)
            val_part[h, at] = val_sum[kind].astype(jnp.bfloat16).reshape(parts, unit, width)

    def head_step(h, carry):
        @pl.when(jnp.logical_and(is_first, h < hpd - 1))
        def _():
            for target in across:
                for which in range(2):
                    fetch(h, target, me, which).wait_send()
                    fetch(h + 1, target, me, which).start()

        each(h, mates, fetch, "arrived")

        @pl.when(is_first)
        def _():
            attend(h, False)

        @pl.when(jnp.logical_not(is_first))
        def _():
            each(h, across, fetch, "arrived")
            attend(h, True)
            each(h, across, give, "start")

        each(h, mates, give, "start")
        key_home[h, me] = key_part[h, me]
        val_home[h, me] = val_part[h, me]
        return carry

    lax.fori_loop(0, hpd, head_step, 0)

    def share(target, source):
        return pltpu.make_async_remote_copy(
            src_ref=sink_part,
            dst_ref=sink_ctx.at[source],
            send_sem=sink_send.at[target],
            recv_sem=sink_recv.at[source],
            device_id={"ctx": target},
            device_id_type=MESH,
        )

    for target in mates + across:
        share(target, me).start()
    sink_ctx[me] = sink_part[...]
    for target in mates + across:
        share(me, target).wait_recv()
    gathered = sink_ctx[0]
    for source in range(1, n_ctx):
        gathered = gathered + sink_ctx[source]
    for at, ax in enumerate(peers):
        sink_peer[2 * at] = gathered
        swap = pltpu.make_async_remote_copy(
            src_ref=sink_peer.at[2 * at],
            dst_ref=sink_peer.at[2 * at + 1],
            send_sem=peer_send.at[at],
            recv_sem=peer_recv.at[at],
            device_id={ax: 1 - lax.axis_index(ax)},
            device_id_type=MESH,
        )
        swap.start()
        swap.wait()
        gathered = gathered + sink_peer[2 * at + 1]
    gs_ref[...] = gathered

    def finish(h, carry):
        each(h, mates, give, "arrived")

        @pl.when(is_first)
        def _():
            each(h, across, give, "arrived")
            for p in range(parts):
                for home, out in ((key_home, gk_ref), (val_home, gv_ref)):
                    a = home[h, slot * parts + p].astype(jnp.float32)
                    b = home[h, other * parts + p].astype(jnp.float32)
                    out[:, cols(p * hpd + h)] = (a + b).astype(jnp.bfloat16)

        @pl.when(jnp.logical_not(is_first))
        def _():
            for p in range(parts):
                for home, out in ((key_home, gk_ref), (val_home, gv_ref)):
                    out[:, cols(p * hpd + h)] = home[h, slot * parts + p]
        return carry

    lax.fori_loop(0, hpd, finish, 0)

    def drain(h, carry):
        @pl.when(jnp.logical_and(is_first, h == hpd - 1))
        def _():
            each(h, across, fetch, "sent")

        @pl.when(jnp.logical_not(is_first))
        def _():
            each(h, across, give, "sent")
        each(h, mates, fetch, "sent")
        each(h, mates, give, "sent")
        return carry

    lax.fori_loop(0, hpd, drain, 0)
    for target in mates + across:
        share(target, me).wait_send()


def two_block_call(first, parts, hpd, q, g, k, v, chosen, sink):
    unit = k.shape[0]
    block = parts * unit
    n_ctx = 2 * parts
    vmem = pl.BlockSpec(memory_space=pltpu.VMEM)
    smem = pl.BlockSpec(memory_space=pltpu.SMEM)
    slots = pltpu.VMEM((hpd, n_ctx, unit, DH), jnp.bfloat16)
    sums = pltpu.VMEM((2, block, DH), jnp.float32)
    dma = pltpu.SemaphoreType.DMA
    bf16 = jnp.bfloat16
    return pl.pallas_call(
        functools.partial(two_block_kernel, first, parts, hpd, unit),
        out_shape=(
            jax.ShapeDtypeStruct(q.shape, bf16),
            jax.ShapeDtypeStruct(q.shape, bf16),
            jax.ShapeDtypeStruct(k.shape, bf16),
            jax.ShapeDtypeStruct(k.shape, bf16),
            jax.ShapeDtypeStruct((8, DH), jnp.float32),
        ),
        in_specs=[vmem, vmem, vmem, vmem, smem, smem],
        out_specs=(vmem,) * 5,
        scratch_shapes=[
            slots, slots, slots, slots, slots, slots, sums, sums,
            pltpu.VMEM((8, DH), jnp.float32),
            pltpu.VMEM((n_ctx, 8, DH), jnp.float32),
            pltpu.VMEM((4, 8, DH), jnp.float32),
            dma((2, hpd, n_ctx)), dma((2, hpd, n_ctx)),
            dma((2, hpd, n_ctx)), dma((2, hpd, n_ctx)),
            dma((n_ctx,)), dma((n_ctx,)), dma((2,)), dma((2,)),
        ],
        compiler_params=pltpu.CompilerParams(
            collective_id=first, has_side_effects=True, vmem_limit_bytes=40 * 1024 * 1024
        ),
        name=f"two_block_{first}",
    )(q, g, k, v, chosen, sink)


def put_kernel(n, *refs):
    sems = refs[-1]
    copies = [pltpu.make_async_copy(refs[i], refs[n + i], sems.at[i]) for i in range(n)]
    for copy in copies:
        copy.start()
    for copy in copies:
        copy.wait()


def put_results(*arrays):
    n = len(arrays)
    anywhere = pl.BlockSpec(memory_space=pl.ANY)
    return pl.pallas_call(
        functools.partial(put_kernel, n),
        out_shape=tuple(jax.ShapeDtypeStruct(a.shape, a.dtype) for a in arrays),
        in_specs=[anywhere] * n,
        out_specs=(anywhere,) * n,
        scratch_shapes=[pltpu.SemaphoreType.DMA((n,))],
        name="put_results",
    )(*arrays)


def two_block_body(query, key, value, grad_out, chosen, placed, sink):
    block = query.shape[3]
    unit = key.shape[1]
    parts = block // unit
    hpd = query.shape[4] // DH
    q = query.reshape(block, hpd * DH)
    g = grad_out.reshape(block, hpd * DH)
    k = key.reshape(unit, -1)
    v = value.reshape(unit, -1)
    att, gq, gk, gv, gs = lax.cond(
        placed[0] == 0,
        functools.partial(two_block_call, 0, parts, hpd),
        functools.partial(two_block_call, 1, parts, hpd),
        q, g, k, v, chosen, sink,
    )
    att, gq, gk, gv = put_results(att, gq, gk, gv)
    return (
        att.reshape(query.shape),
        gq.reshape(query.shape),
        gk.reshape(key.shape),
        gv.reshape(key.shape),
        gs[0, :HEADS],
    )


def body(query, key, value, grad_out, chosen, placed, sink):
    parts = query.shape[3] // key.shape[1]
    if query.shape[0] == 1 and lax.axis_size("ctx") == 2 * parts:
        return two_block_body(query, key, value, grad_out, chosen, placed, sink)
    return general_body(query, key, value, grad_out, chosen, placed, sink)


def solution(mesh):
    in_specs = (
        P("dp", "ctx", "head", None, None),
        P("dp", "ctx", "head"),
        P("dp", "ctx", "head"),
        P("dp", "ctx", "head", None, None),
        P("dp", None, "head", None),
        P(),
        P("head"),
    )
    out_specs = (
        P("dp", "ctx", "head", None, None),
        P("dp", "ctx", "head", None, None),
        P("dp", "ctx", "head"),
        P("dp", "ctx", "head"),
        P(),
    )
    return jax.shard_map(body, mesh=mesh, in_specs=in_specs, out_specs=out_specs, check_vma=False)
```

profile of v0, /device:TPU:0, one launch (start us, length us, event | category | flops | bytes accessed | tf_op | source)
XLA Modules:
  0.0 81.2 jit_solution(14262122970672975820)
XLA Ops:
  0.6 0.0 copy-start.2
  0.6 0.6 copy-done.2
  1.3 0.0 copy-start
  1.3 0.0 copy-start.1
  1.4 0.7 copy-done
  2.0 0.0 copy-done.1
  2.0 77.3 %conditional.1 = ((bf16[512,512]{1,0:T(8,128)(2,1)S(1)}, bf16[512,512]{1,0:T(8,128)(2,1)S(1)}, bf16[128,2048]{1,0:T(8,128)(2,1)S(1)}, bf16[128,2048]{1,0:T(8,128)(2,1)S(1)}, f32[8,128]{1,0:T(8,128)S(1)})) conditional(s32[]{:T(128)} %bitcast, (bf16[512,512]{1,0:T(8,128)(2,1)}, bf16[512,512]{1,0:T(8,128)(2,1)}, bf16[128,2048]{1,0:T(8,128)(2,1)}, ...), branch_computations={%region_0.0_spmd, %region_1.0_spmd} | conditional | bytes 776 | solution.py:491
  2.0 0.1 copy.13.chosen_ref
  2.1 77.2 %two_block_0.1 = (bf16[512,512]{1,0:T(8,128)(2,1)S(1)}, bf16[512,512]{1,0:T(8,128)(2,1)S(1)}, bf16[128,2048]{1,0:T(8,128)(2,1)S(1)}, bf16[128,2048]{1,0:T(8,128)(2,1)S(1)}, f32[8,128]{1,0:T(8,128)S(1)}) custom-call(bf16[512,512]{1,0:T(8,128)(2,1)} %get-tuple-element.47.q_ref, bf16[512,512]{1,0:T(8,128)(2,1)} %get-tuple-element.48.g_ref, ...), custom_call_target="tpu_custom_call" | custom-call | tf_op jit(solution)/shard_map/cond/branch_1_fun/two_block_0/pallas_call | solution.py:433
  79.3 0.5 slice_bitcast_fusion
  79.8 1.3 %put_results.1 = (bf16[512,512]{1,0:T(8,128)(2,1)}, bf16[512,512]{1,0:T(8,128)(2,1)}, bf16[128,2048]{1,0:T(8,128)(2,1)}, bf16[128,2048]{1,0:T(8,128)(2,1)}) custom-call(bf16[512,512]{1,0:T(8,128)(2,1)S(1)} %get-tuple-element.104.refs_0_, bf16[512,512]{1,0:T(8,128)(2,1)S(1)} %get-tuple-element.103.refs_1_, bf16[128,2048]{1,0:T(8,128)(2,1)S(1)} %get-tuple-element.102.refs_2_, ...), custom_call_target="tpu_custom_call" | custom-call | tf_op jit(solution)/shard_map/put_results/pallas_call | solution.py:472
Async XLA Ops:
  0.6 0.7 copy-start.2
  1.3 0.7 copy-start
  1.3 0.7 copy-start.1
where the time goes:
time: 80.4 us; the launch traced here: 81.2 us
  Pallas kernels  78.5 us (98%)
  local copies, waits for them, and re-layouts  1.92 us (2%)
    pallas_call x1, Pallas kernels, two_block_call(): pl.pallas_call(functools.partial(two_block_kernel, first, parts, hpd, uni...  77.2 us

commit v1 on v0

--- a/solution.py
+++ b/solution.py
@@ -229,9 +229,20 @@
                 else:
                     make(h, me, target, which).wait_recv()
 
+    half = parts // 2
+    pieces = 2 * half
+    ahead = pieces - 1
+
+    def piece(h, s):
+        visit, which = half - 1 - s // 2, s % 2
+        targets = [other * parts + visit * 2 + t for t in range(2)]
+        return [fetch(h, target, me, which) for target in targets]
+
     @pl.when(is_first)
     def _():
-        each(0, across, fetch, "start")
+        for s in range(ahead):
+            for copy in piece(0, s):
+                copy.start()
 
     def send_head(h, carry):
         each(h, mates, fetch, "start")
@@ -322,33 +333,6 @@
             key_part[h, at] = key_sum[kind].astype(jnp.bfloat16).reshape(parts, unit, width)
             val_part[h, at] = val_sum[kind].astype(jnp.bfloat16).reshape(parts, unit, width)
 
-    def head_step(h, carry):
-        @pl.when(jnp.logical_and(is_first, h < hpd - 1))
-        def _():
-            for target in across:
-                for which in range(2):
-                    fetch(h, target, me, which).wait_send()
-                    fetch(h + 1, target, me, which).start()
-
-        each(h, mates, fetch, "arrived")
-
-        @pl.when(is_first)
-        def _():
-            attend(h, False)
-
-        @pl.when(jnp.logical_not(is_first))
-        def _():
-            each(h, across, fetch, "arrived")
-            attend(h, True)
-            each(h, across, give, "start")
-
-        each(h, mates, give, "start")
-        key_home[h, me] = key_part[h, me]
-        val_home[h, me] = val_part[h, me]
-        return carry
-
-    lax.fori_loop(0, hpd, head_step, 0)
-
     def share(target, source):
         return pltpu.make_async_remote_copy(
             src_ref=sink_part,
@@ -359,8 +343,47 @@
             device_id_type=MESH,
         )
 
-    for target in mates + across:
-        share(target, me).start()
+    def head_step(h, carry):
+        @pl.when(is_first)
+        def _():
+            for gone, late in zip(piece(h, 0), piece(h, ahead)):
+                gone.wait_send()
+                late.start()
+
+        @pl.when(jnp.logical_and(is_first, h < hpd - 1))
+        def _():
+            for s in range(1, pieces):
+                for gone, late in zip(piece(h, s), piece(h + 1, s - 1)):
+                    gone.wait_send()
+                    late.start()
+
+        each(h, mates, fetch, "arrived")
+
+        @pl.when(is_first)
+        def _():
+            attend(h, False)
+
+        @pl.when(jnp.logical_not(is_first))
+        def _():
+            each(h, across, fetch, "arrived")
+            attend(h, True)
+
+        @pl.when(h == hpd - 1)
+        def _():
+            for target in mates + across:
+                share(target, me).start()
+
+        @pl.when(jnp.logical_not(is_first))
+        def _():
+            each(h, across, give, "start")
+
+        each(h, mates, give, "start")
+        key_home[h, me] = key_part[h, me]
+        val_home[h, me] = val_part[h, me]
+        return carry
+
+    lax.fori_loop(0, hpd, head_step, 0)
+
     sink_ctx[me] = sink_part[...]
     for target in mates + across:
         share(me, target).wait_recv()
@@ -406,7 +429,9 @@
     def drain(h, carry):
         @pl.when(jnp.logical_and(is_first, h == hpd - 1))
         def _():
-            each(h, across, fetch, "sent")
+            for s in range(1, pieces):
+                for copy in piece(h, s):
+                    copy.wait_send()
 
         @pl.when(jnp.logical_not(is_first))
         def _():

time: 80.4 us -> 78.8 us (0.980); the launches traced: 81.2 us -> 78.6 us
  Pallas kernels: 78.5 us -> 76 us
    pallas_call x1, Pallas kernels: 77.2 us -> 74.6 us  [two_block_call(): pl.pallas_call(functools.partial(two_block_kernel, first, parts, hpd, uni...]
where the time goes in v1:
time: 78.8 us; the launch traced here: 78.6 us
  Pallas kernels  76 us (96%)
  local copies, waits for them, and re-layouts  1.92 us (2%)
    pallas_call x1, Pallas kernels, two_block_call(): pl.pallas_call(functools.partial(two_block_kernel, first, parts, hpd, uni...  74.6 us

profile of v1, /device:TPU:0, one launch (start us, length us, event | category | flops | bytes accessed | tf_op | source)
XLA Modules:
  0.0 78.6 jit_solution(10915481453293382261)
XLA Ops:
  0.6 0.0 copy-start.2
  0.6 0.6 copy-done.2
  1.3 0.0 copy-start
  1.3 0.0 copy-start.1
  1.4 0.7 copy-done
  2.0 0.0 copy-done.1
  2.0 74.7 %conditional.1 = ((bf16[512,512]{1,0:T(8,128)(2,1)S(1)}, bf16[512,512]{1,0:T(8,128)(2,1)S(1)}, bf16[128,2048]{1,0:T(8,128)(2,1)S(1)}, bf16[128,2048]{1,0:T(8,128)(2,1)S(1)}, f32[8,128]{1,0:T(8,128)S(1)})) conditional(s32[]{:T(128)} %bitcast, (bf16[512,512]{1,0:T(8,128)(2,1)}, bf16[512,512]{1,0:T(8,128)(2,1)}, bf16[128,2048]{1,0:T(8,128)(2,1)}, ...), branch_computations={%region_0.0_spmd, %region_1.0_spmd} | conditional | bytes 776 | solution.py:516
  2.0 0.1 copy.13.chosen_ref
  2.1 74.6 %two_block_0.1 = (bf16[512,512]{1,0:T(8,128)(2,1)S(1)}, bf16[512,512]{1,0:T(8,128)(2,1)S(1)}, bf16[128,2048]{1,0:T(8,128)(2,1)S(1)}, bf16[128,2048]{1,0:T(8,128)(2,1)S(1)}, f32[8,128]{1,0:T(8,128)S(1)}) custom-call(bf16[512,512]{1,0:T(8,128)(2,1)} %get-tuple-element.47.q_ref, bf16[512,512]{1,0:T(8,128)(2,1)} %get-tuple-element.48.g_ref, ...), custom_call_target="tpu_custom_call" | custom-call | tf_op jit(solution)/shard_map/cond/branch_1_fun/two_block_0/pallas_call | solution.py:458
  76.7 0.5 slice_bitcast_fusion
  77.2 1.3 %put_results.1 = (bf16[512,512]{1,0:T(8,128)(2,1)}, bf16[512,512]{1,0:T(8,128)(2,1)}, bf16[128,2048]{1,0:T(8,128)(2,1)}, bf16[128,2048]{1,0:T(8,128)(2,1)}) custom-call(bf16[512,512]{1,0:T(8,128)(2,1)S(1)} %get-tuple-element.104.refs_0_, bf16[512,512]{1,0:T(8,128)(2,1)S(1)} %get-tuple-element.103.refs_1_, bf16[128,2048]{1,0:T(8,128)(2,1)S(1)} %get-tuple-element.102.refs_2_, ...), custom_call_target="tpu_custom_call" | custom-call | tf_op jit(solution)/shard_map/put_results/pallas_call | solution.py:497
Async XLA Ops:
  0.6 0.7 copy-start.2
  1.3 0.7 copy-start
  1.3 0.7 copy-start.1

commit v2 on v0

--- a/solution.py
+++ b/solution.py
@@ -162,6 +162,7 @@
 
 MESH = pl.DeviceIdType.MESH
 ROWS = 256
+LOG2E = 1.4426950408889634
 
 
 def two_block_kernel(
@@ -229,9 +230,20 @@
                 else:
                     make(h, me, target, which).wait_recv()
 
+    half = parts // 2
+    pieces = 2 * half
+    ahead = pieces - 1
+
+    def piece(h, s):
+        visit, which = half - 1 - s // 2, s % 2
+        targets = [other * parts + visit * 2 + t for t in range(2)]
+        return [fetch(h, target, me, which) for target in targets]
+
     @pl.when(is_first)
     def _():
-        each(0, across, fetch, "start")
+        for s in range(ahead):
+            for copy in piece(0, s):
+                copy.start()
 
     def send_head(h, carry):
         each(h, mates, fetch, "start")
@@ -244,110 +256,6 @@
     lane = lax.broadcasted_iota(jnp.int32, (8, width), 1)
     top_row = lax.broadcasted_iota(jnp.int32, (8, width), 0) == 0
     sink_part[...] = jnp.zeros((8, width), jnp.float32)
-
-    def attend(h, with_other):
-        local_head = pos * hpd + h
-        k_own = keys[h, pl.ds(slot * parts, parts)].reshape(block, width)
-        v_own = vals[h, pl.ds(slot * parts, parts)].reshape(block, width)
-        sink_logit = sink_ref[local_head]
-        segs = [(k_own, v_own, 0)]
-        if with_other:
-            k_oth = keys[h, pl.ds(other * parts, parts)].reshape(block, width)
-            v_oth = vals[h, pl.ds(other * parts, parts)].reshape(block, width)
-            segs.append((k_oth, v_oth, 1))
-            sees = chosen_ref[0, 1, local_head, 0] < 1
-            for entry in range(1, chosen_ref.shape[3]):
-                sees = jnp.logical_or(sees, chosen_ref[0, 1, local_head, entry] < 1)
-            hide = jnp.where(sees, 0.0, -jnp.inf).astype(jnp.float32)
-        sink_total = jnp.zeros((1, 1), jnp.float32)
-        for r in range(block // ROWS):
-            rows = pl.ds(r * ROWS, ROWS)
-            q = q_ref[rows, cols(h)]
-            g = g_ref[rows, cols(h)]
-            used = []
-            top = jnp.full((ROWS, 1), sink_logit, jnp.float32)
-            for k_all, v_all, kind in segs:
-                n = (r + 1) * ROWS if kind == 0 else block
-                k, v = k_all[:n], v_all[:n]
-                s = inner_rows(q, k) * scale
-                if kind == 0:
-                    at_row = lax.broadcasted_iota(jnp.int32, (ROWS, n), 0) + r * ROWS
-                    at_col = lax.broadcasted_iota(jnp.int32, (ROWS, n), 1)
-                    s = jnp.where(at_col <= at_row, s, -jnp.inf)
-                else:
-                    s = s + hide
-                top = jnp.maximum(top, jnp.max(s, axis=1, keepdims=True))
-                used.append((k, v, s, kind, n))
-            sink_exp = jnp.exp(sink_logit - top)
-            total = sink_exp
-            expos = []
-            for k, v, s, kind, n in used:
-                e = jnp.exp(s - top)
-                total = total + jnp.sum(e, axis=1, keepdims=True)
-                expos.append(e)
-            inv = 1.0 / total
-            out = jnp.zeros((ROWS, width), jnp.float32)
-            probs, weights = [], []
-            for (k, v, s, kind, n), e in zip(used, expos):
-                p = e * inv
-                w = p.astype(jnp.bfloat16)
-                out = out + jnp.dot(w, v, preferred_element_type=jnp.float32)
-                probs.append(p)
-                weights.append(w)
-            out = out.astype(jnp.bfloat16)
-            att_ref[rows, cols(h)] = out
-            delta = jnp.sum(g.astype(jnp.float32) * out.astype(jnp.float32), axis=1, keepdims=True)
-            sink_total = sink_total - jnp.sum(sink_exp * inv * delta, axis=0, keepdims=True)
-            gq = jnp.zeros((ROWS, width), jnp.float32)
-            for (k, v, s, kind, n), p, w in zip(used, probs, weights):
-                dprob = inner_rows(g, v)
-                ds = (p * (dprob - delta) * scale).astype(jnp.bfloat16)
-                gq = gq + jnp.dot(ds, k, preferred_element_type=jnp.float32)
-                dk = outer_rows(ds, q)
-                dv = outer_rows(w, g)
-                if r == 0:
-                    key_sum[kind, :n] = dk
-                    val_sum[kind, :n] = dv
-                    if n < block:
-                        key_sum[kind, n:] = jnp.zeros((block - n, width), jnp.float32)
-                        val_sum[kind, n:] = jnp.zeros((block - n, width), jnp.float32)
-                else:
-                    key_sum[kind, :n] += dk
-                    val_sum[kind, :n] += dv
-            gq_ref[rows, cols(h)] = gq.astype(jnp.bfloat16)
-        mine = jnp.logical_and(lane == lax.axis_index("head") * (parts * hpd) + local_head, top_row)
-        sink_part[...] += jnp.where(mine, sink_total, 0.0)
-        for kind, place in ((0, slot), (1, other))[: 2 if with_other else 1]:
-            at = pl.ds(place * parts, parts)
-            key_part[h, at] = key_sum[kind].astype(jnp.bfloat16).reshape(parts, unit, width)
-            val_part[h, at] = val_sum[kind].astype(jnp.bfloat16).reshape(parts, unit, width)
-
-    def head_step(h, carry):
-        @pl.when(jnp.logical_and(is_first, h < hpd - 1))
-        def _():
-            for target in across:
-                for which in range(2):
-                    fetch(h, target, me, which).wait_send()
-                    fetch(h + 1, target, me, which).start()
-
-        each(h, mates, fetch, "arrived")
-
-        @pl.when(is_first)
-        def _():
-            attend(h, False)
-
-        @pl.when(jnp.logical_not(is_first))
-        def _():
-            each(h, across, fetch, "arrived")
-            attend(h, True)
-            each(h, across, give, "start")
-
-        each(h, mates, give, "start")
-        key_home[h, me] = key_part[h, me]
-        val_home[h, me] = val_part[h, me]
-        return carry
-
-    lax.fori_loop(0, hpd, head_step, 0)
 
     def share(target, source):
         return pltpu.make_async_remote_copy(
@@ -359,8 +267,123 @@
             device_id_type=MESH,
         )
 
-    for target in mates + across:
-        share(target, me).start()
+    def keep_part(h, kind, place):
+        at = pl.ds(place * parts, parts)
+        key_part[h, at] = (key_sum[kind] * scale).astype(jnp.bfloat16).reshape(parts, unit, width)
+        val_part[h, at] = val_sum[kind].astype(jnp.bfloat16).reshape(parts, unit, width)
+
+    def back(kind, r, n, q, g, k, v, p, w, delta):
+        ds = (p * (inner_rows(g, v) - delta)).astype(jnp.bfloat16)
+        dk = outer_rows(ds, q)
+        dv = outer_rows(w, g)
+        if r == 0:
+            key_sum[kind, :n] = dk
+            val_sum[kind, :n] = dv
+            if n < block:
+                key_sum[kind, n:] = jnp.zeros((block - n, width), jnp.float32)
+                val_sum[kind, n:] = jnp.zeros((block - n, width), jnp.float32)
+        else:
+            key_sum[kind, :n] += dk
+            val_sum[kind, :n] += dv
+        return jnp.dot(ds, k, preferred_element_type=jnp.float32)
+
+    def attend(h, with_other):
+        local_head = pos * hpd + h
+        k_own = keys[h, pl.ds(slot * parts, parts)].reshape(block, width)
+        v_own = vals[h, pl.ds(slot * parts, parts)].reshape(block, width)
+        sink_logit = sink_ref[local_head] * LOG2E
+        if with_other:
+            k_oth = keys[h, pl.ds(other * parts, parts)].reshape(block, width)
+            v_oth = vals[h, pl.ds(other * parts, parts)].reshape(block, width)
+            sees = chosen_ref[0, 1, local_head, 0] < 1
+            for entry in range(1, chosen_ref.shape[3]):
+                sees = jnp.logical_or(sees, chosen_ref[0, 1, local_head, entry] < 1)
+        sink_total = jnp.zeros((1, 1), jnp.float32)
+        kept = []
+        for r in range(block // ROWS):
+            rows = pl.ds(r * ROWS, ROWS)
+            q = q_ref[rows, cols(h)]
+            g = g_ref[rows, cols(h)]
+            n = (r + 1) * ROWS
+            k, v = k_own[:n], v_own[:n]
+            s = inner_rows(q, k) * (scale * LOG2E)
+            at_row = lax.broadcasted_iota(jnp.int32, (ROWS, n), 0) + r * ROWS
+            at_col = lax.broadcasted_iota(jnp.int32, (ROWS, n), 1)
+            s = jnp.where(at_col <= at_row, s, -jnp.inf)
+            top = jnp.maximum(jnp.max(s, axis=1, keepdims=True), sink_logit)
+            if with_other:
+                s_oth = inner_rows(q, k_oth) * (scale * LOG2E)
+                top_oth = jnp.max(s_oth, axis=1, keepdims=True)
+                top = jnp.maximum(top, jnp.where(sees, top_oth, -jnp.inf))
+                e_oth = jnp.exp2(s_oth - jnp.where(sees, top, jnp.inf))
+            e = jnp.exp2(s - top)
+            sink_exp = jnp.exp2(sink_logit - top)
+            total = sink_exp + jnp.sum(e, axis=1, keepdims=True)
+            if with_other:
+                total = total + jnp.sum(e_oth, axis=1, keepdims=True)
+            inv = 1.0 / total
+            p = e * inv
+            w = p.astype(jnp.bfloat16)
+            out = jnp.dot(w, v, preferred_element_type=jnp.float32)
+            if with_other:
+                p_oth = e_oth * inv
+                w_oth = p_oth.astype(jnp.bfloat16)
+                out = out + jnp.dot(w_oth, v_oth, preferred_element_type=jnp.float32)
+            out = out.astype(jnp.bfloat16)
+            att_ref[rows, cols(h)] = out
+            delta = jnp.sum(g.astype(jnp.float32) * out.astype(jnp.float32), axis=1, keepdims=True)
+            sink_total = sink_total - jnp.sum(sink_exp * inv * delta, axis=0, keepdims=True)
+            gq = jnp.zeros((ROWS, width), jnp.float32)
+            if with_other:
+                gq = back(1, r, block, q, g, k_oth, v_oth, p_oth, w_oth, delta)
+            kept.append((r, n, q, g, k, v, p, w, delta, gq))
+        mine = jnp.logical_and(lane == lax.axis_index("head") * (parts * hpd) + local_head, top_row)
+        sink_part[...] += jnp.where(mine, sink_total, 0.0)
+
+        @pl.when(h == hpd - 1)
+        def _():
+            for target in mates + across:
+                share(target, me).start()
+        if with_other:
+            keep_part(h, 1, other)
+            each(h, across, give, "start")
+        for r, n, q, g, k, v, p, w, delta, gq in kept:
+            gq = gq + back(0, r, n, q, g, k, v, p, w, delta)
+            gq_ref[pl.ds(r * ROWS, ROWS), cols(h)] = (gq * scale).astype(jnp.bfloat16)
+        keep_part(h, 0, slot)
+
+    def head_step(h, carry):
+        @pl.when(is_first)
+        def _():
+            for gone, late in zip(piece(h, 0), piece(h, ahead)):
+                gone.wait_send()
+                late.start()
+
+        @pl.when(jnp.logical_and(is_first, h < hpd - 1))
+        def _():
+            for s in range(1, pieces):
+                for gone, late in zip(piece(h, s), piece(h + 1, s - 1)):
+                    gone.wait_send()
+                    late.start()
+
+        each(h, mates, fetch, "arrived")
+
+        @pl.when(is_first)
+        def _():
+            attend(h, False)
+
+        @pl.when(jnp.logical_not(is_first))
+        def _():
+            each(h, across, fetch, "arrived")
+            attend(h, True)
+
+        each(h, mates, give, "start")
+        key_home[h, me] = key_part[h, me]
+        val_home[h, me] = val_part[h, me]
+        return carry
+
+    lax.fori_loop(0, hpd, head_step, 0)
+
     sink_ctx[me] = sink_part[...]
     for target in mates + across:
         share(me, target).wait_recv()
@@ -406,7 +429,9 @@
     def drain(h, carry):
         @pl.when(jnp.logical_and(is_first, h == hpd - 1))
         def _():
-            each(h, across, fetch, "sent")
+            for s in range(1, pieces):
+                for copy in piece(h, s):
+                    copy.wait_send()
 
         @pl.when(jnp.logical_not(is_first))
         def _():

time: 80.4 us -> 74.4 us (0.925)
  the two profiles are of different devices: /device:TPU:0 before, /device:TPU:24 now
where the time goes in v2:
time: 74.4 us; the launch traced here: 74.2 us
  Pallas kernels  71.6 us (96%)
  local copies, waits for them, and re-layouts  1.92 us (3%)
    pallas_call x1, Pallas kernels, two_block_call(): pl.pallas_call(functools.partial(two_block_kernel, first, parts, hpd, uni...  70.3 us

profile of v2, /device:TPU:24, one launch (start us, length us, event | category | flops | bytes accessed | tf_op | source)
XLA Modules:
  0.0 74.2 jit_solution(10489045339309824966)
XLA Ops:
  0.6 0.0 copy-start.2
  0.6 0.6 copy-done.2
  1.3 0.0 copy-start
  1.3 0.0 copy-start.1
  1.4 0.7 copy-done
  2.0 0.0 copy-done.1
  2.0 70.4 %conditional.1 = ((bf16[512,512]{1,0:T(8,128)(2,1)S(1)}, bf16[512,512]{1,0:T(8,128)(2,1)S(1)}, bf16[128,2048]{1,0:T(8,128)(2,1)S(1)}, bf16[128,2048]{1,0:T(8,128)(2,1)S(1)}, f32[8,128]{1,0:T(8,128)S(1)})) conditional(s32[]{:T(128)} %bitcast, (bf16[512,512]{1,0:T(8,128)(2,1)}, bf16[512,512]{1,0:T(8,128)(2,1)}, bf16[128,2048]{1,0:T(8,128)(2,1)}, ...), branch_computations={%region_0.0_spmd, %region_1.0_spmd} | conditional | bytes 776 | solution.py:516
  2.0 0.1 copy.12.chosen_ref
  2.1 70.3 %two_block_1.1 = (bf16[512,512]{1,0:T(8,128)(2,1)S(1)}, bf16[512,512]{1,0:T(8,128)(2,1)S(1)}, bf16[128,2048]{1,0:T(8,128)(2,1)S(1)}, bf16[128,2048]{1,0:T(8,128)(2,1)S(1)}, f32[8,128]{1,0:T(8,128)S(1)}) custom-call(bf16[512,512]{1,0:T(8,128)(2,1)} %get-tuple-element.41.q_ref, bf16[512,512]{1,0:T(8,128)(2,1)} %get-tuple-element.42.g_ref, ...), custom_call_target="tpu_custom_call" | custom-call | tf_op jit(solution)/shard_map/cond/branch_0_fun/two_block_1/pallas_call | solution.py:458
  72.4 0.5 slice_bitcast_fusion
  72.9 1.3 %put_results.1 = (bf16[512,512]{1,0:T(8,128)(2,1)}, bf16[512,512]{1,0:T(8,128)(2,1)}, bf16[128,2048]{1,0:T(8,128)(2,1)}, bf16[128,2048]{1,0:T(8,128)(2,1)}) custom-call(bf16[512,512]{1,0:T(8,128)(2,1)S(1)} %get-tuple-element.104.refs_0_, bf16[512,512]{1,0:T(8,128)(2,1)S(1)} %get-tuple-element.103.refs_1_, bf16[128,2048]{1,0:T(8,128)(2,1)S(1)} %get-tuple-element.102.refs_2_, ...), custom_call_target="tpu_custom_call" | custom-call | tf_op jit(solution)/shard_map/put_results/pallas_call | solution.py:497
Async XLA Ops:
  0.6 0.7 copy-start.2
  1.3 0.7 copy-start
  1.3 0.7 copy-start.1

commit v3 on v2

--- a/solution.py
+++ b/solution.py
@@ -235,7 +235,9 @@
     ahead = pieces - 1
 
     def piece(h, s):
-        visit, which = half - 1 - s // 2, s % 2
+        visit, which = s // 2, s % 2
+        if first == 0:
+            visit = half - 1 - visit
         targets = [other * parts + visit * 2 + t for t in range(2)]
         return [fetch(h, target, me, which) for target in targets]
 
@@ -246,7 +248,10 @@
                 copy.start()
 
     def send_head(h, carry):
-        each(h, mates, fetch, "start")
+        @pl.when(jnp.logical_or(jnp.logical_not(is_first), h == 0))
+        def _():
+            each(h, mates, fetch, "start")
+
         keys[h, me] = k_ref[:, cols(pos * hpd + h)]
         vals[h, me] = v_ref[:, cols(pos * hpd + h)]
         return carry
@@ -361,6 +366,7 @@
 
         @pl.when(jnp.logical_and(is_first, h < hpd - 1))
         def _():
+            each(h + 1, mates, fetch, "start")
             for s in range(1, pieces):
                 for gone, late in zip(piece(h, s), piece(h + 1, s - 1)):
                     gone.wait_send()

time: 74.4 us -> 74.2 us (level)
  the two profiles are of different devices: /device:TPU:24 before, /device:TPU:0 now
where the time goes in v3:
time: 74.2 us; the launch traced here: 74 us
  Pallas kernels  71.4 us (96%)
  local copies, waits for them, and re-layouts  1.92 us (3%)
    pallas_call x1, Pallas kernels, two_block_call(): pl.pallas_call(functools.partial(two_block_kernel, first, parts, hpd, uni...  70 us

profile of v3, /device:TPU:0, one launch (start us, length us, event | category | flops | bytes accessed | tf_op | source)
XLA Modules:
  0.0 74.0 jit_solution(17969858462989595236)
XLA Ops:
  0.6 0.0 copy-start.2
  0.6 0.6 copy-done.2
  1.3 0.0 copy-start
  1.3 0.0 copy-start.1
  1.4 0.7 copy-done
  2.0 0.0 copy-done.1
  2.0 70.1 %conditional.1 = ((bf16[512,512]{1,0:T(8,128)(2,1)S(1)}, bf16[512,512]{1,0:T(8,128)(2,1)S(1)}, bf16[128,2048]{1,0:T(8,128)(2,1)S(1)}, bf16[128,2048]{1,0:T(8,128)(2,1)S(1)}, f32[8,128]{1,0:T(8,128)S(1)})) conditional(s32[]{:T(128)} %bitcast, (bf16[512,512]{1,0:T(8,128)(2,1)}, bf16[512,512]{1,0:T(8,128)(2,1)}, bf16[128,2048]{1,0:T(8,128)(2,1)}, ...), branch_computations={%region_0.0_spmd, %region_1.0_spmd} | conditional | bytes 776 | solution.py:522
  2.0 0.1 copy.13.chosen_ref
  2.1 70.0 %two_block_0.1 = (bf16[512,512]{1,0:T(8,128)(2,1)S(1)}, bf16[512,512]{1,0:T(8,128)(2,1)S(1)}, bf16[128,2048]{1,0:T(8,128)(2,1)S(1)}, bf16[128,2048]{1,0:T(8,128)(2,1)S(1)}, f32[8,128]{1,0:T(8,128)S(1)}) custom-call(bf16[512,512]{1,0:T(8,128)(2,1)} %get-tuple-element.47.q_ref, bf16[512,512]{1,0:T(8,128)(2,1)} %get-tuple-element.48.g_ref, ...), custom_call_target="tpu_custom_call" | custom-call | tf_op jit(solution)/shard_map/cond/branch_1_fun/two_block_0/pallas_call | solution.py:464
  72.2 0.5 slice_bitcast_fusion
  72.7 1.3 %put_results.1 = (bf16[512,512]{1,0:T(8,128)(2,1)}, bf16[512,512]{1,0:T(8,128)(2,1)}, bf16[128,2048]{1,0:T(8,128)(2,1)}, bf16[128,2048]{1,0:T(8,128)(2,1)}) custom-call(bf16[512,512]{1,0:T(8,128)(2,1)S(1)} %get-tuple-element.104.refs_0_, bf16[512,512]{1,0:T(8,128)(2,1)S(1)} %get-tuple-element.103.refs_1_, bf16[128,2048]{1,0:T(8,128)(2,1)S(1)} %get-tuple-element.102.refs_2_, ...), custom_call_target="tpu_custom_call" | custom-call | tf_op jit(solution)/shard_map/put_results/pallas_call | solution.py:503
Async XLA Ops:
  0.6 0.7 copy-start.2
  1.3 0.7 copy-start
  1.3 0.7 copy-start.1
